TPU v7x, 128 devices: a whole 4x4x4 slice. The times are simulated.
128 devices in a mesh: expert: 32 (over x, z, core), tensor: 4 (over y).
Axes of the slice: x: 4, y: 4, z: 4, core: 2. Of those that a mesh axis runs over, the one named last changes fastest.
Arguments:
- attn_partials: bfloat16 [4, 4096, 7168], P('tensor', 'expert'), may hold values from -3 to 3
- residual: bfloat16 [4096, 7168], P('expert'), may hold values from -22.05 to 22.05
- norm_gain: float32 [7168], P('tensor'), may hold values from 0.1 to 1.9
- gate_up: bfloat16 [64, 7168, 2048], P('expert', 'tensor'), may hold values from -0.0625 to 0.0625
- down: bfloat16 [64, 1024, 7168], P('expert', None, 'tensor'), may hold values from -0.1875 to 0.1875
- expert_ids: int32 [4096, 8], P('expert'), may hold values from 0 to 63, as said below
- gate_ints: int32 [4096, 8], P('expert'), may hold values from 2048 to 4096
Outputs:
- layer_out: bfloat16 [4096, 7168], P('expert', 'tensor')
Inputs may be any that keep to these rules, and one draw needn't show every extreme that they name: `expert_ids`: each row names 8 different experts; among the 128 rows of one index of the expert axis no expert is named more than 24 times, and some expert is named exactly 24 times.
All inputs are finite; a program needn't handle non-finite values.
Results may differ from a plain program's by a relative error of at most 0.028.
Values may be sent and summed in bfloat16 or wider, within the bound.
A program may use at most 192 MiB of HBM per device.

v0:
```python
import jax
import jax.numpy as jnp
from jax import lax
from jax.sharding import PartitionSpec as P


def pair_slots(id_block, experts_all, capacity):
    token_count, top_count = id_block.shape
    flat_ids = id_block.reshape(-1)
    one_hot = (flat_ids[:, None] == jnp.arange(experts_all, dtype=jnp.int32)[None, :]).astype(
        jnp.int32
    )
    running = jnp.cumsum(one_hot, axis=0) - 1
    slot_index = jnp.sum(running * one_hot, axis=1)
    target = flat_ids * capacity + slot_index
    pair_owner = jnp.arange(token_count * top_count, dtype=jnp.int32) // top_count
    slot_token = (
        jnp.full((experts_all * capacity,), token_count, jnp.int32).at[target].set(pair_owner)
    )
    return (target, slot_token)


def per_device(attn_partials, residual, norm_gain, gate_up, down, expert_ids, gate_ints):
    groups = lax.axis_size("expert")
    tensor_ways = lax.axis_size("tensor")
    token_count, model_width = residual.shape
    quarter = model_width // tensor_ways
    local_count = gate_up.shape[0]
    experts_all = local_count * groups
    top_count = expert_ids.shape[1]
    capacity = 3 * token_count * top_count // (2 * experts_all)
    hidden_width = down.shape[1]
    col_start = lax.axis_index("tensor") * quarter
    attention = lax.psum(attn_partials[0], "tensor").astype(jnp.float32)
    stream_wide = (
        (residual.astype(jnp.float32) + attention).astype(jnp.bfloat16).astype(jnp.float32)
    )
    mean_square = jnp.mean(stream_wide * stream_wide, axis=1, keepdims=True)
    stream_part = lax.dynamic_slice_in_dim(stream_wide, col_start, quarter, 1)
    normed = (stream_part * lax.rsqrt(mean_square + 1e-06) * norm_gain[None, :]).astype(
        jnp.bfloat16
    )
    target, slot_token = pair_slots(expert_ids, experts_all, capacity)
    padded = jnp.concatenate([normed, jnp.zeros((1, quarter), jnp.bfloat16)], 0)
    outgoing = padded[slot_token].reshape(groups, local_count, capacity, quarter)
    partial_value = jnp.einsum(
        "send,edf->senf",
        lax.all_to_all(outgoing, "expert", split_axis=0, concat_axis=0, tiled=True),
        gate_up,
        preferred_element_type=jnp.float32,
    )
    summed = lax.psum(partial_value.astype(jnp.bfloat16), "tensor").astype(jnp.float32)
    hidden = (jax.nn.silu(summed[..., :hidden_width]) * summed[..., hidden_width:]).astype(
        jnp.bfloat16
    )
    result = jnp.einsum("senf,efd->send", hidden, down, preferred_element_type=jnp.float32).astype(
        jnp.bfloat16
    )
    returned = lax.all_to_all(result, "expert", split_axis=0, concat_axis=0, tiled=True)
    flat_back = returned.reshape(experts_all * capacity, quarter)
    gathered = flat_back[target].reshape(token_count, top_count, quarter)
    gate_float = gate_ints.astype(jnp.float32)
    gates = 2.5 * gate_float / jnp.sum(gate_float, axis=1, keepdims=True)
    routed_sum = jnp.sum(gates[:, :, None] * gathered.astype(jnp.float32), axis=1)
    return (stream_part + routed_sum).astype(jnp.bfloat16)


def solution(mesh):
    in_specs = (
        P("tensor", "expert", None),
        P("expert", None),
        P("tensor"),
        P("expert", "tensor", None),
        P("expert", None, "tensor"),
        P("expert", None),
        P("expert", None),
    )
    out_specs = P("expert", "tensor")
    return jax.shard_map(
        per_device, mesh=mesh, in_specs=in_specs, out_specs=out_specs, check_vma=False
    )
```

profile of v0, /device:TPU:1, one launch (start us, length us, event | category | flops | bytes accessed | tf_op | source)
XLA Modules:
  0.0 408.8 jit_solution(4575411784336823149)
XLA Ops:
  6.5 0.7 all-reduce.4.cloned.1.call-update
  7.3 0.0 all-reduce.6.cloned.1.call-start
  7.3 0.8 copy.19
  8.1 0.1 eq.29
  8.2 0.1 eq.25
  8.3 18.0 %reduce-window.6 = s32[64,8,128]{2,1,0:T(8,128)S(1)} reduce-window(s32[64,8,128]{2,1,0:T(8,128)S(1)} %fusion.18, s32[]{:T(128)} %constant.18.clone.1), window={size=1x1x128 pad=0_0x0_0x127_0}, to_apply=%region_3.4 | reduce-window | flops 8323072 | bytes 524292 | tf_op jit(solution)/shard_map/reduce-window
  26.3 0.1 slice.20
  26.5 0.1 copy.21
  26.7 0.1 copy.22
  26.7 0.7 broadcast_multiply_fusion
  27.4 0.1 copy.18
  27.5 0.1 mul.73
  27.7 0.1 add_add_fusion
  27.8 0.1 fusion.17
  27.9 4.3 %scatter_custom_fusion = s32[1536]{0:T(1024)S(1)} fusion(s32[1024]{0:T(1024)S(1)} %bitcast.45, s32[1024]{0:T(1024)S(1)} %add_select_fusion, s32[]{:T(128)} %constant.48.clone.1), kind=kCustom, calls=%fused_computation.36 | custom fusion | bytes 6148 | tf_op jit(solution)/shard_map/scatter | solution.py:18
  32.2 35.2 %all-reduce.4.cloned.1.call-done = bf16[128,7168]{1,0:T(8,128)(2,1)} async-done(((bf16[128,7168]{1,0:T(8,128)(2,1)}), bf16[128,7168]{1,0:T(8,128)(2,1)}) %all-reduce.4.cloned.1.call-update) | async-done | bytes 1835024 | tf_op jit(solution)/shard_map/psum | solution.py:34
  67.4 2.2 multiply_reduce_fusion
  69.6 1.8 copy-done
  71.4 0.1 multiply_convert_fusion
  71.6 6.7 %gather_fusion = bf16[1536,1792]{1,0:T(8,128)(2,1)} fusion(bf16[129,1792]{1,0:T(8,128)(2,1)S(1)} %concatenate.3, s32[2048]{0:T(1024)S(1)} %pad_clamp_fusion), kind=kCustom, calls=%fused_computation | custom fusion | bytes 11016192 | tf_op jit(solution)/shard_map/gather | solution.py:45
  78.3 72.8 %all_to_all.10 = bf16[32,2,24,1792]{3,2,1,0:T(8,128)(2,1)S(1)} all-to-all(bf16[32,2,24,1792]{3,2,1,0:T(8,128)(2,1)} %bitcast.40), channel_id=1, replica_groups=mesh['expert'=32,'tensor'=4] {'expert'}, dimensions={0} | all-to-all | bytes 11010048 | tf_op jit(solution)/shard_map/all_to_all | solution.py:48
  151.2 16.4 %convert_bitcast_fusion = bf16[32,2,24,2048]{3,2,0,1:T(8,128)(2,1)} fusion(bf16[2,1792,2048]{2,1,0:T(8,128)(2,1)} %param.10, bf16[32,2,24,1792]{3,2,1,0:T(8,128)(2,1)S(1)} %all_to_all.10), kind=kOutput, calls=%fused_computation.11 | convolution fusion | flops 11277434880 | bytes 26476544 | tf_op jit(solution)/shard_map/send,edf->senf/dot_general | solution.py:46
  167.6 122.8 %all-reduce.6.cloned.1.call-done = bf16[32,2,24,2048]{3,2,0,1:T(8,128)(2,1)} async-done(((bf16[32,2,24,2048]{3,2,0,1:T(8,128)(2,1)}), bf16[32,2,24,2048]{3,2,0,1:T(8,128)(2,1)}) %all-reduce.6.cloned.1.call-update) | async-done | bytes 6291472 | tf_op jit(solution)/shard_map/psum | solution.py:52
  290.4 4.2 %convert_element_type.59 = f32[32,2,24,2048]{3,2,0,1:T(8,128)S(1)} convert(bf16[32,2,24,2048]{3,2,0,1:T(8,128)(2,1)} %all-reduce.6.cloned.1.call-done) | non-fusion elementwise | flops 3145728 | bytes 18874368 | tf_op jit(solution)/shard_map/convert_element_type | solution.py:52
  294.7 9.7 %convert_bitcast_fusion.1 = bf16[32,2,24,1792]{3,2,0,1:T(8,128)(2,1)S(1)} fusion(bf16[2,1024,1792]{2,1,0:T(8,128)(2,1)} %param.11, f32[32,2,24,2048]{3,2,0,1:T(8,128)S(1)} %convert_element_type.59), kind=kOutput, calls=%fused_computation.13 | convolution fusion | flops 5649334272 | bytes 25427968 | tf_op jit(solution)/shard_map/senf,efd->send/dot_general | solution.py:56
  304.4 2.9 copy.24
  307.3 7.9 %all-to-all-start.1 = ((bf16[32,2,24,1792]{3,2,1,0:T(8,128)(2,1)}), bf16[32,2,24,1792]{3,2,1,0:T(8,128)(2,1)}, u32[]{:S(2)}, u32[]{:S(2)}) async-start(bf16[32,2,24,1792]{3,2,1,0:T(8,128)(2,1)} %copy.24), calls=%async_computation.1 | async-start | bytes 11010048 | tf_op jit(solution)/shard_map/all_to_all | solution.py:59
  315.2 0.1 copy.17
  315.4 67.9 %all-to-all-done.1 = bf16[32,2,24,1792]{3,2,1,0:T(8,128)(2,1)} async-done(((bf16[32,2,24,1792]{3,2,1,0:T(8,128)(2,1)}), bf16[32,2,24,1792]{3,2,1,0:T(8,128)(2,1)}, u32[]{:S(2)}, u32[]{:S(2)}) %all-to-all-start.1) | async-done | bytes 5505056 | tf_op jit(solution)/shard_map/all_to_all | solution.py:59
  383.3 11.2 %gather_fusion.1 = bf16[1024,1792]{1,0:T(8,128)(2,1)} fusion(bf16[1536,1792]{1,0:T(8,128)(2,1)} %bitcast.12, s32[1024]{0:T(1024)S(1)} %broadcast_clamp_fusion), kind=kCustom, calls=%fused_computation.1 | custom fusion | bytes 7344128 | tf_op jit(solution)/shard_map/gather | solution.py:61
  394.5 5.3 %fusion.2 = f32[128,1792]{1,0:T(8,128)S(1)} fusion(bf16[1024,1792]{1,0:T(8,128)(2,1)} %gather_fusion.1, f32[128,8]{1,0:T(8,128)S(1)} %copy.17), kind=kLoop, calls=%fused_computation.6 | loop fusion | flops 5275648 | bytes 4591616 | tf_op jit(solution)/shard_map/reduce_sum | solution.py:64
  399.9 2.1 add_convert_fusion.1
  (21 shorter events, 0.2 us)
Async XLA Ops:
  6.5 60.9 %copy-start.1 = (bf16[128,7168]{1,0:T(8,128)(2,1)S(1)}, bf16[128,7168]{1,0:T(8,128)(2,1)}, u32[]{:S(2)}) copy-start(bf16[128,7168]{1,0:T(8,128)(2,1)} %param.8) | copy-start | bytes 5505028
  6.5 60.9 %all-reduce.4.cloned.1.call-start = ((), (), s32[]{:S(2)}) async-start(), calls=%async_computation.2 | async-start | bytes 3670016 | tf_op jit(solution)/shard_map/psum | solution.py:34
  7.3 64.2 %copy-start.3 = (f32[1792]{0:T(1024)S(1)}, f32[1792]{0:T(1024)}, u32[]{:S(2)}) copy-start(f32[1792]{0:T(1024)} %param.9) | copy-start | bytes 21508
  7.3 283.2 %all-reduce.6.cloned.1.call-start = ((), (), s32[]{:S(2)}) async-start(), calls=%async_computation.3 | async-start | bytes 12582912 | tf_op jit(solution)/shard_map/psum | solution.py:52
  69.6 1.8 copy-start
  307.3 7.9 %copy-start.2 = (s32[128,8]{0,1:T(8,128)S(1)}, s32[128,8]{0,1:T(8,128)}, u32[]{:S(2)}) copy-start(s32[128,8]{0,1:T(8,128)} %param.13) | copy-start | bytes 12292
  307.3 76.0 %all-to-all-start.1 = ((bf16[32,2,24,1792]{3,2,1,0:T(8,128)(2,1)}), bf16[32,2,24,1792]{3,2,1,0:T(8,128)(2,1)}, u32[]{:S(2)}, u32[]{:S(2)}) async-start(bf16[32,2,24,1792]{3,2,1,0:T(8,128)(2,1)} %copy.24), calls=%async_computation.1 | async-start | bytes 11010048 | tf_op jit(solution)/shard_map/all_to_all | solution.py:59
Sparse Core Ops, SparseCore 0:
  9.7 57.6 all-reduce.3
  167.8 122.6 all-reduce.5
where the time goes:
time: 415 us; the launch traced here: 409 us
  waiting for transfers between devices  227 us (55%)
  blocking collectives  72.8 us (18%)
  other arithmetic  33 us (8%)
  local copies, waits for them, and re-layouts  28.6 us (7%)
  matrix products  26.2 us (6%)
  between operations  13.6 us (3%)
  starting transfers between devices  7.94 us (2%)
    psum x1, waiting for transfers between devices, per_device(): lax.psum(partial_value.astype(jnp.bfloat16), 'tensor').astype(jnp.float32)  123 us
    all_to_all x1, blocking collectives, per_device(): lax.all_to_all(outgoing, 'expert', split_axis=0, concat_axis=0, tiled=True)  72.8 us
    all_to_all x1, waiting for transfers between devices, per_device(): lax.all_to_all(result, 'expert', split_axis=0, concat_axis=0, tiled=True)  67.9 us
    psum x1, waiting for transfers between devices, per_device(): attention = lax.psum(attn_partials[0], 'tensor').astype(jnp.float32)  35.2 us
    another operation x2, other arithmetic  18 us
    dot_general x1, matrix products, per_device(): jnp.einsum('send,edf->senf', lax.all_to_all(outgoing, 'expert', split_axi...  16.4 us
    gather x1, local copies, waits for them, and re-layouts, per_device(): gathered = flat_back[target].reshape(token_count, top_count, quarter)  11.2 us
    dot_general x1, matrix products, per_device(): jnp.einsum('senf,efd->send', hidden, down, preferred_element_type=jnp.flo...  9.74 us
  transfers between devices with their start and end apart: 3, of which 3 were waited for; matrix products, arithmetic and copies ran while one was open for 6% of the time, Pallas kernels for 0%

commit v1 on v0

v1 whole, which is shorter than its diff:
```python
import functools
import jax
import jax.numpy as jnp
import numpy as np
from jax import lax
from jax.experimental import pallas as pl
from jax.experimental.pallas import tpu as pltpu
from jax.sharding import PartitionSpec as P

MESH = pl.DeviceIdType.MESH
F32, BF16 = jnp.float32, jnp.bfloat16
DZ = (0, 2, 1, 3)
STEP_DX = (0, 1, 3, 1, 3, 2, 2, 0)
STEP_PAIR = (1, 1, 1, 0, 0, 1, 0, 0)
STEPS = 8
META = 128


def lut(index, values):
    result = jnp.int32(values[0])
    for at, value in enumerate(values):
        if at:
            result = jnp.where(index == at, jnp.int32(value), result)
    return result


def row_table(cap):
    table = np.full((8, 8 * cap), -1e6, np.float32)
    for l in range(2):
        for q in range(2):
            for j in range(cap):
                for s in range(2):
                    table[2 * q + s, ((l * 2 + s) * 2 + q) * cap + j] = l * cap + j
                table[4 + q, (l * 2 + q) * cap + j] = l * cap + j
    return table


def layer_kernel(
    cap,
    attn,
    resid,
    gain,
    wgu,
    wdn,
    ids,
    ints,
    tab,
    out,
    wg,
    wd,
    toks,
    pb,
    xb,
    yr,
    hb,
    ob,
    pr,
    own,
    cs,
    zr,
    xr,
    ar,
    stream,
    ssb,
    w_sem,
    l_sem,
    ar_s,
    ar_r,
    ss_s,
    ss_r,
    agz_s,
    agx_s,
    ag_r,
    core_s,
    core_r,
    y_s,
    y_r,
    h_s,
    h_r,
    p_s,
    p_r,
    z_s,
    z_r,
    x_s,
    x_r,
):
    e = lax.axis_index("expert")
    y = lax.axis_index("tensor")
    x, z, c = e // 8, lax.rem(e // 2, 4), lax.rem(e, 2)
    tokens, quarter = stream.shape
    top = ids.shape[1]
    width = 4 * quarter
    half_rows = 4 * cap
    block = hb.shape[3]

    def at(dx=0, dz=0, dc=0, dy=0):
        ex = (lax.rem(x + dx, 4) * 4 + lax.rem(z + dz, 4)) * 2 + lax.rem(c + dc, 2)
        return (ex, lax.rem(y + dy, 4))

    def remote(src, dst, ssem, rsem, dev):
        return pltpu.make_async_remote_copy(
            src_ref=src, dst_ref=dst, send_sem=ssem, recv_sem=rsem, device_id=dev, device_id_type=MESH
        )

    def cols(start, size):
        return pl.ds(pl.multiple_of(start * size, size), size)

    def attn_copy(d):
        return remote(
            attn.at[:, cols(lax.rem(y + d, 4), quarter)], ar.at[d - 1], ar_s.at[d - 1], ar_r.at[d - 1], at(dy=d)
        )

    for d in (1, 3, 2):
        attn_copy(d).start()
    mine = pltpu.make_async_copy(attn.at[:, cols(y, quarter)], cs.at[0, 0], l_sem.at[0])
    rest = pltpu.make_async_copy(resid.at[:, cols(y, quarter)], cs.at[0, 1], l_sem.at[1])
    mine.start()
    rest.start()

    def weight_copies():
        copies = []
        for l in range(2):
            for o in range(4):
                for g in range(2):
                    copies.append(
                        pltpu.make_async_copy(
                            wgu.at[l, :, pl.ds(g * 4 * block + o * block, block)],
                            wg.at[l, o, :, pl.ds(g * block, block)],
                            w_sem.at[(l * 4 + o) * 2 + g],
                        )
                    )
            copies.append(pltpu.make_async_copy(wdn.at[l], wd.at[l], w_sem.at[16 + l]))
        return copies

    for copy in weight_copies():
        copy.start()

    lane = lax.broadcasted_iota(jnp.int32, (tokens, META), 1)
    row = lax.broadcasted_iota(jnp.int32, (tokens, META), 0)
    id_block = ids[...]
    hits = jnp.zeros((tokens, META), F32)
    for k in range(top):
        hits = hits + jnp.where(id_block[:, k : k + 1] == lane, 1.0, 0.0)
    before = jnp.where(lane < row, 1.0, 0.0).astype(BF16)
    count = jnp.dot(before, hits.astype(BF16), preferred_element_type=F32)
    gate_float = ints[...].astype(F32)
    gates = 2.5 * gate_float / jnp.sum(gate_float, axis=1, keepdims=True)
    meta = jnp.zeros((tokens, META), F32)
    for k in range(top):
        this = id_block[:, k : k + 1]
        slot = jnp.sum(jnp.where(this == lane, count, 0.0), axis=1, keepdims=True)
        meta = jnp.where(lane == k, this.astype(F32), meta)
        meta = jnp.where(lane == top + k, slot, meta)
        meta = jnp.where(lane == 2 * top + k, gates[:, k : k + 1], meta)
    toks[0, 0, c, :, pl.ds(quarter, META)] = meta.astype(BF16)

    mine.wait()
    rest.wait()
    for d in (1, 3, 2):
        attn_copy(d).wait_recv()
    attention = cs[0, 0].astype(F32) + ar[0].astype(F32) + ar[1].astype(F32) + ar[2].astype(F32)
    summed = (cs[0, 1].astype(F32) + attention).astype(BF16)
    stream[...] = summed
    wide = summed.astype(F32)
    ssb[0] = jnp.broadcast_to(jnp.sum(wide * wide, axis=1, keepdims=True), (tokens, META))

    def ss_copy(d):
        return remote(ssb.at[0], ssb.at[d], ss_s.at[d - 1], ss_r.at[d - 1], at(dy=d))

    for d in (1, 3, 2):
        ss_copy(d).start()
    for d in (1, 3, 2):
        ss_copy(d).wait_recv()
    total = (ssb[0] + ssb[1] + ssb[2] + ssb[3])[:, :1]
    wide = stream[...].astype(F32)
    normed = wide * lax.rsqrt(total / width + 1e-06) * gain[...]
    toks[0, 0, c, :, pl.ds(0, quarter)] = normed.astype(BF16)

    def agz_copy(p):
        dz = DZ[p]
        there = DZ.index((4 - dz) % 4)
        return remote(toks.at[0, 0, c], toks.at[0, there, c], agz_s.at[p], ag_r.at[0, there], at(dz=dz))

    def agx_copy(p, dx):
        return remote(toks.at[0, p, c], toks.at[4 - dx, p, c], agx_s.at[p, dx], ag_r.at[4 - dx, p], at(dx=dx))

    def arrival(dx, p):
        return remote(toks.at[dx, p, c], toks.at[dx, p, c], agz_s.at[0], ag_r.at[dx, p], at(dc=1))

    def core_copy(dx, p):
        return remote(toks.at[dx, p, c], toks.at[dx, p, c], core_s.at[dx, p], core_r.at[dx, p], at(dc=1))

    def core_arrival(dx, p):
        there = toks.at[dx, p, 1 - c]
        return remote(there, there, core_s.at[dx, p], core_r.at[dx, p], at(dc=1))

    agz_copy(2).start()
    agz_copy(3).start()
    agx_copy(0, 1).start()
    agx_copy(0, 3).start()
    agz_copy(1).start()
    for p in (2, 3):
        arrival(0, p).wait_recv()
        core_copy(0, p).start()
        agx_copy(p, 1).start()
        agx_copy(p, 3).start()
    for copy in weight_copies():
        copy.wait()

    def codes_of(dx, p, s):
        m = toks[dx, p, s, :, pl.ds(quarter, META)].astype(F32)
        return m[:, :top] * cap + m[:, top : 2 * top], m[:, 2 * top : 3 * top]

    def y_copy(j, d):
        return remote(
            pb.at[lax.rem(j, 2), lax.rem(y + d, 4)],
            yr.at[lax.rem(j, 4), d - 1],
            y_s.at[lax.rem(j, 2), d - 1],
            y_r.at[lax.rem(j, 4), d - 1],
            at(dy=d),
        )

    def h_copy(j, d):
        spot = hb.at[lax.rem(j, 4), y]
        return remote(spot, spot, h_s.at[lax.rem(j, 4), d - 1], h_r.at[lax.rem(j, 4), d - 1], at(dy=d))

    def h_arrival(j, d):
        spot = hb.at[lax.rem(j, 4), lax.rem(y + 4 - d, 4)]
        return remote(spot, spot, h_s.at[lax.rem(j, 4), d - 1], h_r.at[lax.rem(j, 4), d - 1], at(dy=d))

    def p_copy(j):
        return remote(
            ob.at[lax.rem(j, 2), :, 1 - c],
            pr.at[lax.rem(j, 4)],
            p_s.at[lax.rem(j, 2)],
            p_r.at[lax.rem(j, 4)],
            at(dc=1),
        )

    def z_copy(j, dx, q, dz):
        return remote(cs.at[lax.rem(j, 2), q], zr.at[dx, dz - 1], z_s.at[lax.rem(j, 2), q], z_r.at[dx, dz - 1], at(dz=dz))

    def x_copy(dx):
        return remote(own.at[dx], xr.at[dx - 1], x_s.at[dx - 1], x_r.at[dx - 1], at(dx=dx))

    def project(j):
        dx, p0 = lut(j, STEP_DX), 2 * lut(j, STEP_PAIR)
        core_arrival(dx, p0).wait_recv()
        core_arrival(dx, p0 + 1).wait_recv()
        picks = []
        for q in range(2):
            for s in range(2):
                codes, _ = codes_of(dx, p0 + q, s)
                rows = tab[2 * q + s : 2 * q + s + 1, :] + (2 * cap * e).astype(F32)
                pick = jnp.zeros((tokens, 8 * cap), F32)
                for k in range(top):
                    pick = jnp.where(codes[:, k : k + 1] == rows, 1.0, pick)
                picks.append(pick)
        pick = jnp.concatenate(picks, axis=0).astype(BF16)

        @pl.loop(0, quarter // 256)
        def _(n):
            data = toks[dx, pl.ds(p0, 2), :, :, cols(n, 256)].reshape(4 * tokens, 256)
            xb[:, cols(n, 256)] = lax.dot_general(
                pick, data, (((0,), (0,)), ((), ())), preferred_element_type=F32
            ).astype(BF16)

        for l in range(2):

            @pl.loop(0, 4)
            def _(o):
                pb[lax.rem(j, 2), o, pl.ds(l * half_rows, half_rows), :] = jnp.dot(
                    xb[pl.ds(l * half_rows, half_rows), :], wg[l, o], preferred_element_type=F32
                ).astype(BF16)

        for d in (1, 3, 2):
            y_copy(j, d).start()

    def service(j):
        dx, p0 = lut(j, STEP_DX), 2 * lut(j, STEP_PAIR)
        for q in range(2):

            @pl.when(dx != 0)
            def _():
                arrival(dx, p0 + q).wait_recv()

            core_copy(dx, p0 + q).start()

    def activate(j):
        for d in (1, 3, 2):
            y_copy(j, d).wait()
        slot = lax.rem(j, 4)
        value = pb[lax.rem(j, 2), y].astype(F32)
        for d in range(3):
            value = value + yr[slot, d].astype(F32)
        hb[slot, y] = (jax.nn.silu(value[:, :block]) * value[:, block:]).astype(BF16)
        for d in (1, 3, 2):
            h_copy(j, d).start()

    def expand(j):
        for d in (1, 3, 2):
            h_copy(j, d).wait_send()
            h_arrival(j, d).wait_recv()
        slot = lax.rem(j, 4)
        for l in range(2):

            @pl.loop(0, quarter // 256)
            def _(n):
                acc = jnp.zeros((half_rows, 256), F32)
                for o in range(4):
                    acc = acc + jnp.dot(
                        hb[slot, o, pl.ds(l * half_rows, half_rows), :],
                        wd[l, pl.ds(o * block, block), cols(n, 256)],
                        preferred_element_type=F32,
                    )
                ob[lax.rem(j, 2), l, :, :, cols(n, 256)] = acc.astype(BF16).reshape(2, 2 * cap, 256)

        p_copy(j).start()

    def gather_back(j):
        dx, pair = lut(j, STEP_DX), lut(j, STEP_PAIR)
        p_copy(j).wait()

        @pl.when(j >= 2)
        def _():
            before_pair = lut(j - 2, STEP_PAIR)

            @pl.when(before_pair == 1)
            def _():
                z_copy(j, 0, 0, 1).wait_send()

            z_copy(j, 0, 1, 1).wait_send()

        for q in range(2):
            codes, gate = codes_of(dx, 2 * pair + q, c)
            sides = []
            for base in (e, e + 1 - 2 * c):
                rows = tab[4 + q : 5 + q, : 4 * cap] + (2 * cap * base).astype(F32)
                side = jnp.zeros((tokens, 4 * cap), F32)
                for k in range(top):
                    side = jnp.where(codes[:, k : k + 1] == rows, gate[:, k : k + 1], side)
                sides.append(side.astype(BF16))

            def block_of(n):
                here = ob[lax.rem(j, 2), :, c, :, cols(n, 256)].reshape(4 * cap, 256)
                other = pr[lax.rem(j, 4), :, :, cols(n, 256)].reshape(4 * cap, 256)
                value = jnp.dot(sides[0], here, preferred_element_type=F32)
                return (value + jnp.dot(sides[1], other, preferred_element_type=F32)).astype(BF16)

            if q == 0:

                @pl.when(pair == 0)
                def _():
                    @pl.loop(0, quarter // 256)
                    def _(n):
                        own[dx, :, cols(n, 256)] = block_of(n)

                @pl.when(pair == 1)
                def _():
                    @pl.loop(0, quarter // 256)
                    def _(n):
                        cs[lax.rem(j, 2), 0, :, cols(n, 256)] = block_of(n)

                    z_copy(j, dx, 0, 1).start()

            else:

                @pl.loop(0, quarter // 256)
                def _(n):
                    cs[lax.rem(j, 2), 1, :, cols(n, 256)] = block_of(n)

                z_copy(j, dx, 1, jnp.where(pair == 0, 2, 3)).start()

    def combine(dx):
        value = own[dx].astype(F32)
        for dz in (1, 2, 3):
            remote(zr.at[dx, dz - 1], zr.at[dx, dz - 1], z_s.at[0, 0], z_r.at[dx, dz - 1], at(dz=dz)).wait_recv()
            value = value + zr[dx, dz - 1].astype(F32)
        return value

    @pl.loop(0, STEPS + 3)
    def _(it):
        @pl.when(it < STEPS)
        def _():
            project(it)

        @pl.when(it == 0)
        def _():
            arrival(0, 1).wait_recv()
            agx_copy(1, 1).start()
            agx_copy(1, 3).start()

        @pl.when(it == 1)
        def _():
            agx_copy(2, 2).start()

        @pl.when(it == 2)
        def _():
            agx_copy(3, 2).start()

        @pl.when(it == 3)
        def _():
            agx_copy(0, 2).start()
            agx_copy(1, 2).start()

        @pl.when(it + 1 < STEPS)
        def _():
            service(it + 1)

        @pl.when((it >= 1) & (it <= STEPS))
        def _():
            activate(it - 1)

        @pl.when((it >= 2) & (it <= STEPS + 1))
        def _():
            expand(it - 2)

        @pl.when(it >= 3)
        def _():
            gather_back(it - 3)

        @pl.when(it >= 8)
        def _():
            dx = lut(it - 8, (1, 3, 2))
            own[dx] = combine(dx).astype(BF16)
            x_copy(dx).start()

    value = stream[...].astype(F32) + combine(0)
    for dx in (1, 3, 2):
        x_copy(dx).wait()
        value = value + xr[dx - 1].astype(F32)
    out[...] = value.astype(BF16)

    for d in (1, 2, 3):
        attn_copy(d).wait_send()
        ss_copy(d).wait_send()
    for p in (1, 2, 3):
        agz_copy(p).wait_send()
    for p in range(4):
        for dx in range(4):
            if dx:
                agx_copy(p, dx).wait_send()
            core_copy(dx, p).wait_send()
    for j in (STEPS - 2, STEPS - 1):
        z_copy(j, 0, 1, 1).wait_send()


def per_device(attn_partials, residual, norm_gain, gate_up, down, expert_ids, gate_ints):
    tokens, width = residual.shape
    quarter = norm_gain.shape[0]
    local, _, double = gate_up.shape
    hidden = down.shape[1]
    block = hidden // 4
    groups = lax.axis_size("expert")
    top = expert_ids.shape[1]
    cap = 3 * tokens * top // (2 * groups * local)
    rows = 8 * cap
    dma = pltpu.SemaphoreType.DMA
    vmem = pl.BlockSpec(memory_space=pltpu.VMEM)
    anywhere = pl.BlockSpec(memory_space=pl.ANY)
    scratch = [
        pltpu.VMEM((local, 4, quarter, 2 * block), BF16),
        pltpu.VMEM((local, hidden, quarter), BF16),
        pltpu.VMEM((4, 4, 2, tokens, quarter + META), BF16),
        pltpu.VMEM((2, 4, rows, 2 * block), BF16),
        pltpu.VMEM((rows, quarter), BF16),
        pltpu.VMEM((4, 3, rows, 2 * block), BF16),
        pltpu.VMEM((4, 4, rows, block), BF16),
        pltpu.VMEM((2, local, 2, 2 * cap, quarter), BF16),
        pltpu.VMEM((4, local, 2 * cap, quarter), BF16),
        pltpu.VMEM((4, tokens, quarter), BF16),
        pltpu.VMEM((2, 2, tokens, quarter), BF16),
        pltpu.VMEM((4, 3, tokens, quarter), BF16),
        pltpu.VMEM((3, tokens, quarter), BF16),
        pltpu.VMEM((3, tokens, quarter), BF16),
        pltpu.VMEM((tokens, quarter), BF16),
        pltpu.VMEM((4, tokens, META), F32),
        dma((18,)),
        dma((2,)),
        dma((3,)),
        dma((3,)),
        dma((3,)),
        dma((3,)),
        dma((4,)),
        dma((4, 4)),
        dma((4, 4)),
        dma((4, 4)),
        dma((4, 4)),
        dma((2, 3)),
        dma((4, 3)),
        dma((4, 3)),
        dma((4, 3)),
        dma((2,)),
        dma((4,)),
        dma((2, 2)),
        dma((4, 3)),
        dma((3,)),
        dma((3,)),
    ]
    return pl.pallas_call(
        functools.partial(layer_kernel, cap),
        out_shape=jax.ShapeDtypeStruct((tokens, quarter), BF16),
        in_specs=[anywhere, anywhere, vmem, anywhere, anywhere, vmem, vmem, vmem],
        out_specs=vmem,
        scratch_shapes=scratch,
        compiler_params=pltpu.CompilerParams(has_side_effects=True, vmem_limit_bytes=62 * 2**20),
        cost_estimate=pl.CostEstimate(flops=30 * 10**9, bytes_accessed=30 * 10**6, transcendentals=0),
    )(
        attn_partials[0],
        residual,
        norm_gain[None, :],
        gate_up,
        down,
        expert_ids,
        gate_ints,
        jnp.asarray(row_table(cap)),
    )


def solution(mesh):
    in_specs = (
        P("tensor", "expert", None),
        P("expert", None),
        P("tensor"),
        P("expert", "tensor", None),
        P("expert", None, "tensor"),
        P("expert", None),
        P("expert", None),
    )
    return jax.shard_map(
        per_device, mesh=mesh, in_specs=in_specs, out_specs=P("expert", "tensor"), check_vma=False
    )
```

time: 415 us -> 242 us (0.58)
  Pallas kernels: 0 us -> 231 us
  waiting for transfers between devices: 227 us -> 0 us
  blocking collectives: 72.8 us -> 0 us
  other arithmetic: 33 us -> 0 us
  matrix products: 26.2 us -> 0 us
  local copies, waits for them, and re-layouts: 28.6 us -> 5.93 us
  between operations: 13.6 us -> 0.01 us
  starting transfers between devices: 7.94 us -> 0 us
    pallas_call x0 -> x1, Pallas kernels: none -> 231 us  [per_device(): pl.pallas_call(functools.partial(layer_kernel, cap), out_shape=jax.ShapeD...]
    psum x2 -> x0, waiting for transfers between devices: 158 us -> none  [the longest x1 123 us: per_device(): lax.psum(partial_value.astype(jnp.bfloat16), 'tensor').astype(jnp.float32)]
    all_to_all x1 -> x0, blocking collectives: 72.8 us -> none  [per_device(): lax.all_to_all(outgoing, 'expert', split_axis=0, concat_axis=0, tiled=True)]
    all_to_all x1 -> x0, waiting for transfers between devices: 67.9 us -> none  [per_device(): lax.all_to_all(result, 'expert', split_axis=0, concat_axis=0, tiled=True)]
    dot_general x2 -> x0, matrix products: 26.2 us -> none  [the longest x1 16.4 us: per_device(): jnp.einsum('send,edf->senf', lax.all_to_all(outgoing, 'expert', split_axi...]
    another operation x2 -> x0, other arithmetic: 18 us -> none
    gather x2 -> x0, local copies, waits for them, and re-layouts: 18 us -> none  [the longest x1 11.2 us: per_device(): gathered = flat_back[target].reshape(token_count, top_count, quarter)]
    all_to_all x1 -> x0, starting transfers between devices: 7.9 us -> none  [per_device(): lax.all_to_all(result, 'expert', split_axis=0, concat_axis=0, tiled=True)]
  transfers between devices with their start and end apart: 3 -> 0, of which waited for: 3 -> 0; matrix products, arithmetic and copies ran while one was open for 6% -> 0% of each run, Pallas kernels for 0% -> 0%
where the time goes in v1:
time: 242 us; the launch traced here: 237 us
  Pallas kernels  231 us (95%)
  local copies, waits for them, and re-layouts  5.93 us (2%)
    pallas_call x1, Pallas kernels, per_device(): pl.pallas_call(functools.partial(layer_kernel, cap), out_shape=jax.ShapeD...  231 us

profile of v1, /device:TPU:1, one launch (start us, length us, event | category | flops | bytes accessed | tf_op | source)
XLA Modules:
  0.0 237.3 jit_solution(5088531481591079344)
XLA Ops:
  0.0 1.3 broadcast_in_dim.3.gain
  1.3 1.4 copy.9.ids
  2.7 1.4 copy.10.ints
  4.1 231.4 %shard_map.82 = bf16[128,1792]{1,0:T(8,128)(2,1)} custom-call(bf16[128,7168]{1,0:T(8,128)(2,1)} %bitcast.1, bf16[128,7168]{1,0:T(8,128)(2,1)} %resid.1, f32[1,1792]{1,0:T(1,128)} %broadcast_in_dim.3.gain, bf16[2,1792,2048]{2,1,0:T(8,128)(2,1)} %wgu.1, bf16[2,1024,1792]{2,1,0:T(8,128)(2,1)} %wdn.1, s32[128,8]{1,0:T(8,128)} %copy.9.ids, s32[128,8]{1,0:T(8,128)} %copy.10.ints, ...), custom_call_target="tpu_custom_call" | custom-call | flops 30000001024 | bytes 30000000 | tf_op jit(solution)/shard_map/pallas_call | solution.py:500
  235.5 1.8 copy.12

commit v2 on v1

v2 whole, which is shorter than its diff:
```python
import functools
import jax
import jax.numpy as jnp
import numpy as np
from jax import lax
from jax.experimental import pallas as pl
from jax.experimental.pallas import tpu as pltpu
from jax.sharding import PartitionSpec as P

MESH = pl.DeviceIdType.MESH
F32, BF16 = jnp.float32, jnp.bfloat16
CHIP_DX = (0, 0, 1, 3, 1, 3, 1, 3, 2, 2, 1, 3, 2, 2, 0, 0)
CHIP_DZ = (1, 3, 0, 0, 1, 3, 3, 1, 1, 3, 2, 2, 0, 2, 0, 2)
STEPS = 8
META = 128


def lut(index, values):
    result = jnp.int32(values[0])
    for at, value in enumerate(values):
        if at:
            result = jnp.where(index == at, jnp.int32(value), result)
    return result


def row_table(cap):
    table = np.full((8, 4 * cap), -1e6, np.float32)
    for l in range(2):
        for q in range(2):
            for j in range(cap):
                table[q, (l * 2 + q) * cap + j] = l * cap + j
    return table


def layer_kernel(
    cap,
    experts_all,
    attn,
    resid,
    gain,
    wgu,
    wdn,
    ids,
    ints,
    tab,
    out,
    wg,
    wd,
    toks,
    rowc,
    pb,
    xb,
    y1,
    y2,
    hb,
    ob,
    pr,
    own,
    cs,
    fr,
    sr,
    stream,
    ssb,
    w_sem,
    l_sem,
    a1_s,
    a1_r,
    a2_s,
    a2_r,
    ss_s,
    ss_r,
    ag1_s,
    ag1_r,
    ag2_s,
    ag2_r,
    agf_s,
    agf_r,
    core_s,
    core_r,
    y1_s,
    y1_r,
    y2_s,
    y2_r,
    h_s,
    h_r,
    p_s,
    p_r,
    f_s,
    f_r,
    s_s,
    s_r,
):
    e = lax.axis_index("expert")
    y = lax.axis_index("tensor")
    x, z, c = e // 8, lax.rem(e // 2, 4), lax.rem(e, 2)
    tokens, quarter = stream.shape
    top = ids.shape[0]
    width = 4 * quarter
    half_rows = 4 * cap
    block = hb.shape[3]

    def at(dx=0, dz=0, dc=0, dy=0):
        ex = (lax.rem(x + dx, 4) * 4 + lax.rem(z + dz, 4)) * 2 + lax.rem(c + dc, 2)
        return (ex, lax.rem(y + dy, 4))

    def remote(src, dst, ssem, rsem, dev):
        return pltpu.make_async_remote_copy(
            src_ref=src, dst_ref=dst, send_sem=ssem, recv_sem=rsem, device_id=dev, device_id_type=MESH
        )

    def cols(start, size):
        return pl.ds(pl.multiple_of(start * size, size), size)

    barrier = pltpu.get_barrier_semaphore()
    peers = [at(dy=d) for d in (1, 2, 3)] + [at(dx=d) for d in (1, 2, 3)] + [at(dz=d) for d in (1, 2, 3)] + [at(dc=1)]
    for peer in peers:
        pl.semaphore_signal(barrier, inc=1, device_id=peer, device_id_type=MESH)
    pl.semaphore_wait(barrier, len(peers))

    half = tokens // 2

    def attn_first(side):
        rows = pl.ds(side * half, half)
        source = attn.at[rows, cols(lax.rem(y + 2, 4), quarter)]
        return remote(source, fr.at[1, 2, rows], a1_s.at[side], a1_r.at[side], at(dy=1 + 2 * side))

    def attn_second(side):
        return remote(cs.at[1, side], fr.at[1, side], a2_s.at[side], a2_r.at[side], at(dy=1 + 2 * side))

    attn_first(0).start()
    attn_first(1).start()
    beside = [
        pltpu.make_async_copy(attn.at[:, cols(lax.rem(y + 1 + 2 * side, 4), quarter)], cs.at[1, side], l_sem.at[side])
        for side in range(2)
    ]
    mine = pltpu.make_async_copy(attn.at[:, cols(y, quarter)], cs.at[0, 0], l_sem.at[2])
    rest = pltpu.make_async_copy(resid.at[:, cols(y, quarter)], cs.at[0, 1], l_sem.at[3])
    for copy in (*beside, mine, rest):
        copy.start()

    def weight_copies():
        copies = []
        for l in range(2):
            for o in range(4):
                for g in range(2):
                    copies.append(
                        pltpu.make_async_copy(
                            wgu.at[l, :, pl.ds(g * 4 * block + o * block, block)],
                            wg.at[l, o, :, pl.ds(g * block, block)],
                            w_sem.at[(l * 4 + o) * 2 + g],
                        )
                    )
            copies.append(pltpu.make_async_copy(wdn.at[l], wd.at[l], w_sem.at[16 + l]))
        return copies

    for copy in weight_copies():
        copy.start()
    for side in range(2):
        rows = pl.ds(side * half, half)
        beside[side].wait()
        attn_first(side).wait_recv()
        value = cs[1, side, rows, :].astype(F32) + fr[1, 2, rows, :].astype(F32)
        cs[1, side, rows, :] = value.astype(BF16)
        attn_second(side).start()

    experts = lax.broadcasted_iota(jnp.int32, (experts_all, tokens), 0)
    pick_row = lax.broadcasted_iota(jnp.int32, (top, tokens), 0)
    id_block = ids[...]
    hits = jnp.zeros((experts_all, tokens), F32)
    for k in range(top):
        hits = hits + jnp.where(id_block[k : k + 1, :] == experts, 1.0, 0.0)
    earlier = lax.broadcasted_iota(jnp.int32, (tokens, tokens), 0) < lax.broadcasted_iota(jnp.int32, (tokens, tokens), 1)
    count = jnp.dot(hits.astype(BF16), jnp.where(earlier, 1.0, 0.0).astype(BF16), preferred_element_type=F32)
    slots = jnp.zeros((top, tokens), F32)
    for k in range(top):
        slot = jnp.sum(jnp.where(id_block[k : k + 1, :] == experts, count, 0.0), axis=0, keepdims=True)
        slots = jnp.where(pick_row == k, slot, slots)
    gate_float = ints[...].astype(F32)
    gates = 2.5 * gate_float / jnp.sum(gate_float, axis=0, keepdims=True)
    rest_rows = jnp.zeros((META - 3 * top, tokens), F32)
    meta = jnp.concatenate([id_block.astype(F32), slots, gates, rest_rows], axis=0)
    toks[0, 0, c, :, pl.ds(quarter, META)] = meta.T.astype(BF16)

    r = lax.broadcasted_iota(jnp.int32, (8 * cap, tokens), 0)
    l_of = (r >= 4 * cap).astype(jnp.int32)
    r = r - 4 * cap * l_of
    s_of = (r >= 2 * cap).astype(jnp.int32)
    r = r - 2 * cap * s_of
    q_of = (r >= cap).astype(jnp.int32)
    code = (r - cap * q_of + cap * l_of + 2 * cap * e).astype(F32)
    for q in range(2):
        for s in range(2):
            rowc[2 * q + s] = jnp.where((q_of == q) & (s_of == s), code, -1e6)

    mine.wait()
    rest.wait()
    attn_second(0).wait_recv()
    attn_second(1).wait_recv()
    attention = cs[0, 0].astype(F32) + fr[1, 0].astype(F32) + fr[1, 1].astype(F32)
    summed = (cs[0, 1].astype(F32) + attention).astype(BF16)
    stream[...] = summed
    wide = summed.astype(F32)
    ssb[0] = jnp.broadcast_to(jnp.sum(wide * wide, axis=1, keepdims=True), (tokens, META))

    def ss_copy(d):
        return remote(ssb.at[0], ssb.at[d], ss_s.at[d - 1], ss_r.at[d - 1], at(dy=d))

    for d in (1, 3, 2):
        ss_copy(d).start()
    for d in (1, 3, 2):
        ss_copy(d).wait_recv()
    total = (ssb[0] + ssb[1] + ssb[2] + ssb[3])[:, :1]
    wide = stream[...].astype(F32)
    normed = wide * lax.rsqrt(total / width + 1e-06) * gain[...].reshape(1, quarter)
    toks[0, 0, c, :, pl.ds(0, quarter)] = normed.astype(BF16)

    def turned(a, b):
        return a * c + b * (1 - c), a * (1 - c) + b * c

    def spot(a, b):
        dx, dz = turned(a, b)
        return toks.at[dx, dz, c]

    def toward(a, b):
        dx, dz = turned(a, b)
        return at(dx=dx, dz=dz)

    def ag_first(a):
        return remote(spot(0, 0), spot(4 - a, 0), ag1_s.at[a], ag1_r.at[4 - a], toward(a, 0))

    def ag_second(a, b):
        return remote(spot(a, 0), spot(a, 4 - b), ag2_s.at[a, b], ag2_r.at[a, 4 - b], toward(0, b))

    def pass_on(a, side):
        rows = pl.ds(side * half, half)
        return remote(
            spot(a, 3 - 2 * side).at[rows],
            spot(a, 2).at[rows],
            agf_s.at[a, side],
            agf_r.at[a, side],
            toward(0, 1 + 2 * side),
        )

    def core_copy(dx, dz):
        return remote(toks.at[dx, dz, c], toks.at[dx, dz, c], core_s.at[dx, dz], core_r.at[dx, dz], at(dc=1))

    def core_arrival(dx, dz):
        there = toks.at[dx, dz, 1 - c]
        return remote(there, there, core_s.at[dx, dz], core_r.at[dx, dz], at(dc=1))

    def chip(j, q):
        return lut(2 * j + q, CHIP_DX), lut(2 * j + q, CHIP_DZ)

    def service(j):
        for q in range(2):
            dx, dz = chip(j, q)
            a, b = turned(dx, dz)

            @pl.when(b == 2)
            def _():
                pass_on(a, 0).wait_recv()
                pass_on(a, 1).wait_recv()

            @pl.when(lax.rem(b, 2) == 1)
            def _():
                ag_second(a, 4 - b).wait_recv()

            core_copy(dx, dz).start()

    ag_first(1).start()
    ag_first(3).start()
    ag_second(0, 1).start()
    ag_second(0, 3).start()
    for a in (1, 3):
        ag_first(a).wait_recv()
        ag_second(4 - a, 1).start()
        ag_second(4 - a, 3).start()
    ag_first(2).start()
    attn_second(0).wait_send()
    attn_second(1).wait_send()
    service(0)
    for copy in weight_copies():
        copy.wait()

    def y1_copy(j, side):
        n = lax.rem(j, 3)
        return remote(
            pb.at[n, lax.rem(y + 2, 4), pl.ds(side * half_rows, half_rows)],
            y1.at[lax.rem(j, 4), side],
            y1_s.at[n, side],
            y1_r.at[lax.rem(j, 4), side],
            at(dy=1 + 2 * side),
        )

    def y2_copy(j, side):
        n = lax.rem(j, 3)
        return remote(
            pb.at[n, lax.rem(y + 1 + 2 * side, 4)],
            y2.at[lax.rem(j, 4), side],
            y2_s.at[n, side],
            y2_r.at[lax.rem(j, 4), side],
            at(dy=1 + 2 * side),
        )

    def h_copy(j, d):
        spot = hb.at[lax.rem(j, 4), y]
        return remote(spot, spot, h_s.at[lax.rem(j, 4), d - 1], h_r.at[lax.rem(j, 4), d - 1], at(dy=d))

    def h_arrival(j, d):
        spot = hb.at[lax.rem(j, 4), lax.rem(y + 4 - d, 4)]
        return remote(spot, spot, h_s.at[lax.rem(j, 4), d - 1], h_r.at[lax.rem(j, 4), d - 1], at(dy=d))

    def p_copy(j):
        return remote(
            ob.at[lax.rem(j, 2), :, 1 - c],
            pr.at[lax.rem(j, 4)],
            p_s.at[lax.rem(j, 2)],
            p_r.at[lax.rem(j, 4)],
            at(dc=1),
        )

    def first_copy(j, q, outer, inner):
        dev = at(dx=inner * c, dz=inner * (1 - c))
        return remote(cs.at[lax.rem(j, 3), q], fr.at[outer, inner - 1], f_s.at[lax.rem(j, 3), q], f_r.at[outer, inner - 1], dev)

    def second_copy(outer):
        dev = at(dx=outer * (1 - c), dz=outer * c)
        return remote(own.at[outer], sr.at[outer - 1], s_s.at[outer - 1], s_r.at[outer - 1], dev)

    def place(j, q):
        dx, dz = chip(j, q)
        return jnp.where(c == 0, dx, dz), jnp.where(c == 0, dz, dx)

    def project(j):
        chips = [chip(j, q) for q in range(2)]
        core_arrival(*chips[0]).wait_recv()
        core_arrival(*chips[1]).wait_recv()
        picks = []
        for q in range(2):
            for s in range(2):
                m = toks[chips[q][0], chips[q][1], s, :, pl.ds(quarter, META)].astype(F32).T
                codes = m[:top] * cap + m[top : 2 * top]
                pick = jnp.zeros((8 * cap, tokens), F32)
                for k in range(top):
                    pick = jnp.where(rowc[2 * q + s] == codes[k : k + 1, :], 1.0, pick)
                picks.append(pick.astype(BF16))
        picks = [jnp.concatenate(picks[:2], axis=1), jnp.concatenate(picks[2:], axis=1)]

        @pl.loop(0, 2)
        def _(n):
            part = cols(n, quarter // 2)
            value = jnp.zeros((8 * cap, quarter // 2), F32)
            for q in range(2):
                data = toks[chips[q][0], chips[q][1], :, :, part].reshape(2 * tokens, quarter // 2)
                value = value + jnp.dot(picks[q], data, preferred_element_type=F32)
            xb[:, part] = value.astype(BF16)

        for l in range(2):

            @pl.loop(0, 4)
            def _(o):
                pb[lax.rem(j, 3), o, pl.ds(l * half_rows, half_rows), :] = jnp.dot(
                    xb[pl.ds(l * half_rows, half_rows), :], wg[l, o], preferred_element_type=F32
                ).astype(BF16)

        y1_copy(j, 0).start()
        y1_copy(j, 1).start()

    def relay(j):
        n = lax.rem(j, 3)
        for side in range(2):
            y1_copy(j, side).wait()
            o = lax.rem(y + 1 + 2 * side, 4)
            rows = pl.ds(side * half_rows, half_rows)
            value = pb[n, o, rows, :].astype(F32) + y1[lax.rem(j, 4), side].astype(F32)
            pb[n, o, rows, :] = value.astype(BF16)
            y2_copy(j, side).start()

    def activate(j):
        y2_copy(j, 0).wait()
        y2_copy(j, 1).wait()
        slot = lax.rem(j, 4)
        value = pb[lax.rem(j, 3), y].astype(F32) + y2[slot, 0].astype(F32) + y2[slot, 1].astype(F32)
        hb[slot, y] = (jax.nn.silu(value[:, :block]) * value[:, block:]).astype(BF16)
        for d in (1, 3, 2):
            h_copy(j, d).start()

    def expand(j):
        for d in (1, 3, 2):
            h_copy(j, d).wait_send()
            h_arrival(j, d).wait_recv()
        slot = lax.rem(j, 4)
        for l in range(2):
            lhs = jnp.concatenate([hb[slot, o, pl.ds(l * half_rows, half_rows), :] for o in range(4)], axis=1)

            @pl.loop(0, 2)
            def _(n):
                value = jnp.dot(lhs, wd[l, :, cols(n, quarter // 2)], preferred_element_type=F32)
                ob[lax.rem(j, 2), l, :, :, cols(n, quarter // 2)] = value.astype(BF16).reshape(2, 2 * cap, quarter // 2)

        p_copy(j).start()

    def gather_back(j):
        p_copy(j).wait()
        for q in range(2):
            _, inner_before = place(j - 3, q)

            @pl.when((j >= 3) & (inner_before != 0))
            def _():
                first_copy(j, q, 0, 1).wait_send()

        for q in range(2):
            dx, dz = chip(j, q)
            m = toks[dx, dz, c, :, pl.ds(quarter, META)].astype(F32)
            codes, gate = m[:, :top] * cap + m[:, top : 2 * top], m[:, 2 * top : 3 * top]
            sides = []
            for base in (e, e + 1 - 2 * c):
                rows = tab[q : q + 1, :] + (2 * cap * base).astype(F32)
                side = jnp.zeros((tokens, 4 * cap), F32)
                for k in range(top):
                    side = jnp.where(codes[:, k : k + 1] == rows, gate[:, k : k + 1], side)
                sides.append(side.astype(BF16))

            @pl.loop(0, 2)
            def _(n):
                part = cols(n, quarter // 2)
                here = ob[lax.rem(j, 2), :, c, :, part].reshape(4 * cap, quarter // 2)
                other = pr[lax.rem(j, 4), :, :, part].reshape(4 * cap, quarter // 2)
                value = jnp.dot(sides[0], here, preferred_element_type=F32)
                value = value + jnp.dot(sides[1], other, preferred_element_type=F32)
                cs[lax.rem(j, 3), q, :, part] = value.astype(BF16)

            outer, inner = place(j, q)

            @pl.when(inner == 0)
            def _():
                own[outer] = cs[lax.rem(j, 3), q]

            @pl.when(inner != 0)
            def _():
                first_copy(j, q, outer, inner).start()

    def combine(outer):
        value = own[outer].astype(F32)
        for inner in (1, 2, 3):
            first_copy(0, 0, outer, inner).wait_recv()
            value = value + fr[outer, inner - 1].astype(F32)
        return value

    def finish(outer):
        own[outer] = combine(outer).astype(BF16)
        second_copy(outer).start()

    @pl.loop(0, STEPS + 4)
    def _(it):
        @pl.when(it < STEPS)
        def _():
            project(it)

        @pl.when((it >= 1) & (it <= STEPS))
        def _():
            relay(it - 1)

        @pl.when((it >= 2) & (it <= STEPS + 1))
        def _():
            activate(it - 2)

        @pl.when(it == 1)
        def _():
            ag_first(2).wait_recv()
            ag_second(2, 1).start()
            ag_second(2, 3).start()
            pass_on(0, 0).start()
            pass_on(0, 1).start()

        @pl.when(it + 1 < STEPS)
        def _():
            service(it + 1)

        @pl.when(it == 2)
        def _():
            for a in (1, 3):
                pass_on(a, 0).start()
                pass_on(a, 1).start()

        @pl.when(it == 4)
        def _():
            pass_on(2, 0).start()
            pass_on(2, 1).start()

        @pl.when((it >= 3) & (it <= STEPS + 2))
        def _():
            expand(it - 3)

        @pl.when(it >= 4)
        def _():
            gather_back(it - 4)

        @pl.when((c == 1) & (it == 10))
        def _():
            finish(1)
            finish(3)

    @pl.when(c == 0)
    def _():
        finish(1)
        finish(3)

    finish(2)
    value = stream[...].astype(F32) + combine(0)
    for outer in (1, 3, 2):
        second_copy(outer).wait()
        value = value + sr[outer - 1].astype(F32)
    out[...] = value.astype(BF16)

    for side in range(2):
        attn_first(side).wait_send()
    for d in (1, 2, 3):
        ss_copy(d).wait_send()
        ag_first(d).wait_send()
    for a in range(4):
        ag_second(a, 1).wait_send()
        ag_second(a, 3).wait_send()
        pass_on(a, 0).wait_send()
        pass_on(a, 1).wait_send()
        for b in range(4):
            core_copy(a, b).wait_send()
    for j in (STEPS - 3, STEPS - 2, STEPS - 1):
        for q in range(2):
            _, inner = place(j, q)

            @pl.when(inner != 0)
            def _():
                first_copy(j, q, 0, 1).wait_send()


def per_device(attn_partials, residual, norm_gain, gate_up, down, expert_ids, gate_ints):
    tokens, width = residual.shape
    quarter = norm_gain.shape[0]
    local, _, double = gate_up.shape
    hidden = down.shape[1]
    block = hidden // 4
    groups = lax.axis_size("expert")
    top = expert_ids.shape[1]
    cap = 3 * tokens * top // (2 * groups * local)
    rows = 8 * cap
    dma = pltpu.SemaphoreType.DMA
    vmem = pl.BlockSpec(memory_space=pltpu.VMEM)
    anywhere = pl.BlockSpec(memory_space=pl.ANY)
    scratch = [
        pltpu.VMEM((local, 4, quarter, 2 * block), BF16),
        pltpu.VMEM((local, hidden, quarter), BF16),
        pltpu.VMEM((4, 4, 2, tokens, quarter + META), BF16),
        pltpu.VMEM((4, rows, tokens), F32),
        pltpu.VMEM((3, 4, rows, 2 * block), BF16),
        pltpu.VMEM((rows, quarter), BF16),
        pltpu.VMEM((4, 2, rows // 2, 2 * block), BF16),
        pltpu.VMEM((4, 2, rows, 2 * block), BF16),
        pltpu.VMEM((4, 4, rows, block), BF16),
        pltpu.VMEM((2, local, 2, 2 * cap, quarter), BF16),
        pltpu.VMEM((4, local, 2 * cap, quarter), BF16),
        pltpu.VMEM((4, tokens, quarter), BF16),
        pltpu.VMEM((3, 2, tokens, quarter), BF16),
        pltpu.VMEM((4, 3, tokens, quarter), BF16),
        pltpu.VMEM((3, tokens, quarter), BF16),
        pltpu.VMEM((tokens, quarter), BF16),
        pltpu.VMEM((4, tokens, META), F32),
        dma((18,)),
        dma((4,)),
        dma((2,)),
        dma((2,)),
        dma((2,)),
        dma((2,)),
        dma((3,)),
        dma((3,)),
        dma((4,)),
        dma((4,)),
        dma((4, 4)),
        dma((4, 4)),
        dma((4, 2)),
        dma((4, 2)),
        dma((4, 4)),
        dma((4, 4)),
        dma((3, 2)),
        dma((4, 2)),
        dma((3, 2)),
        dma((4, 2)),
        dma((4, 3)),
        dma((4, 3)),
        dma((2,)),
        dma((4,)),
        dma((3, 2)),
        dma((4, 3)),
        dma((3,)),
        dma((3,)),
    ]
    return pl.pallas_call(
        functools.partial(layer_kernel, cap, groups * local),
        out_shape=jax.ShapeDtypeStruct((tokens, quarter), BF16),
        in_specs=[anywhere, anywhere, vmem, anywhere, anywhere, vmem, vmem, vmem],
        out_specs=vmem,
        scratch_shapes=scratch,
        compiler_params=pltpu.CompilerParams(collective_id=0, has_side_effects=True, vmem_limit_bytes=62 * 2**20),
        cost_estimate=pl.CostEstimate(flops=30 * 10**9, bytes_accessed=30 * 10**6, transcendentals=0),
    )(
        attn_partials[0],
        residual,
        norm_gain,
        gate_up,
        down,
        expert_ids.T,
        gate_ints.T,
        jnp.asarray(row_table(cap)),
    )


def solution(mesh):
    in_specs = (
        P("tensor", "expert", None),
        P("expert", None),
        P("tensor"),
        P("expert", "tensor", None),
        P("expert", None, "tensor"),
        P("expert", None),
        P("expert", None),
    )
    return jax.shard_map(
        per_device, mesh=mesh, in_specs=in_specs, out_specs=P("expert", "tensor"), check_vma=False
    )
```

time: 242 us -> 182 us (0.75); the launches traced: 237 us -> 181 us
  Pallas kernels: 231 us -> 179 us
  local copies, waits for them, and re-layouts: 5.93 us -> 1.82 us
    pallas_call x1, Pallas kernels: 231 us -> 179 us  [per_device(): pl.pallas_call(functools.partial(layer_kernel, cap, groups * local), out_...]
    unnamed x3 -> x1, local copies, waits for them, and re-layouts: 4.63 us -> 1.82 us
where the time goes in v2:
time: 182 us; the launch traced here: 181 us
  Pallas kernels  179 us (98%)
  local copies, waits for them, and re-layouts  1.82 us (1%)
    pallas_call x1, Pallas kernels, per_device(): pl.pallas_call(functools.partial(layer_kernel, cap, groups * local), out_...  179 us

profile of v2, /device:TPU:1, one launch (start us, length us, event | category | flops | bytes accessed | tf_op | source)
XLA Modules:
  0.0 181.3 jit_solution(2913736804189138222)
XLA Ops:
  0.0 179.5 %shard_map.82 = bf16[128,1792]{1,0:T(8,128)(2,1)} custom-call(bf16[128,7168]{1,0:T(8,128)(2,1)} %bitcast.3, bf16[128,7168]{1,0:T(8,128)(2,1)} %resid.1, f32[1792]{0:T(1024)} %gain.1, bf16[2,1792,2048]{2,1,0:T(8,128)(2,1)} %wgu.1, bf16[2,1024,1792]{2,1,0:T(8,128)(2,1)} %wdn.1, s32[8,128]{1,0:T(8,128)} %bitcast.4, s32[8,128]{1,0:T(8,128)} %bitcast.5, ...), custom_call_target="tpu_custom_call" | custom-call | flops 30000001024 | bytes 30000000 | tf_op jit(solution)/shard_map/pallas_call | solution.py:597
  179.5 1.8 %copy.10 = bf16[128,1792]{1,0:T(8,128)(2,1)} copy(bf16[128,1792]{1,0:T(8,128)(2,1)} %shard_map.82) | data formatting | bytes 917504

commit v3 on v2

--- a/solution.py
+++ b/solution.py
@@ -9,8 +9,8 @@
 
 MESH = pl.DeviceIdType.MESH
 F32, BF16 = jnp.float32, jnp.bfloat16
-CHIP_DX = (0, 0, 1, 3, 1, 3, 1, 3, 2, 2, 1, 3, 2, 2, 0, 0)
-CHIP_DZ = (1, 3, 0, 0, 1, 3, 3, 1, 1, 3, 2, 2, 0, 2, 0, 2)
+CHIP_DX = (0, 0, 1, 3, 1, 3, 1, 3, 1, 3, 2, 2, 2, 2, 0, 0)
+CHIP_DZ = (1, 3, 0, 0, 1, 3, 3, 1, 2, 2, 1, 3, 2, 0, 2, 0)
 STEPS = 8
 META = 128
 
@@ -261,7 +261,7 @@
                 pass_on(a, 0).wait_recv()
                 pass_on(a, 1).wait_recv()
 
-            @pl.when(lax.rem(b, 2) == 1)
+            @pl.when((lax.rem(b, 2) == 1) & (a != 0))
             def _():
                 ag_second(a, 4 - b).wait_recv()
 
@@ -273,12 +273,15 @@
     ag_second(0, 3).start()
     for a in (1, 3):
         ag_first(a).wait_recv()
-        ag_second(4 - a, 1).start()
-        ag_second(4 - a, 3).start()
-    ag_first(2).start()
+        ag_second(0, a).wait_recv()
     attn_second(0).wait_send()
     attn_second(1).wait_send()
     service(0)
+    service(1)
+    for a in (1, 3):
+        ag_second(a, 1).start()
+        ag_second(a, 3).start()
+    ag_first(2).start()
     for copy in weight_copies():
         copy.wait()
 
@@ -461,7 +464,7 @@
         def _():
             relay(it - 1)
 
-        @pl.when((it >= 2) & (it <= STEPS + 1))
+        @pl.when((it >= 3) & (it <= STEPS + 1))
         def _():
             activate(it - 2)
 
@@ -473,9 +476,13 @@
             pass_on(0, 0).start()
             pass_on(0, 1).start()
 
-        @pl.when(it + 1 < STEPS)
+        @pl.when((it >= 1) & (it + 1 < STEPS))
         def _():
             service(it + 1)
+
+        @pl.when(it == 1)
+        def _():
+            activate(0)
 
         @pl.when(it == 2)
         def _():
@@ -496,12 +503,12 @@
         def _():
             gather_back(it - 4)
 
-        @pl.when((c == 1) & (it == 10))
+        @pl.when((c == 0) & (it == 10))
         def _():
             finish(1)
             finish(3)
 
-    @pl.when(c == 0)
+    @pl.when(c == 1)
     def _():
         finish(1)
         finish(3)

time: 182 us -> 175 us (0.962)
  Pallas kernels: 179 us -> 173 us
    pallas_call x1, Pallas kernels: 179 us -> 173 us  [per_device(): pl.pallas_call(functools.partial(layer_kernel, cap, groups * local), out_...]
where the time goes in v3:
time: 175 us
  Pallas kernels  173 us (99%)
  local copies, waits for them, and re-layouts  1.82 us (1%)
    pallas_call x1, Pallas kernels, per_device(): pl.pallas_call(functools.partial(layer_kernel, cap, groups * local), out_...  173 us

profile of v3, /device:TPU:1, one launch (start us, length us, event | category | flops | bytes accessed | tf_op | source)
XLA Modules:
  0.0 174.9 jit_solution(18227899422917486189)
XLA Ops:
  0.0 173.1 %shard_map.82 = bf16[128,1792]{1,0:T(8,128)(2,1)} custom-call(bf16[128,7168]{1,0:T(8,128)(2,1)} %bitcast.3, bf16[128,7168]{1,0:T(8,128)(2,1)} %resid.1, f32[1792]{0:T(1024)} %gain.1, bf16[2,1792,2048]{2,1,0:T(8,128)(2,1)} %wgu.1, bf16[2,1024,1792]{2,1,0:T(8,128)(2,1)} %wdn.1, s32[8,128]{1,0:T(8,128)} %bitcast.4, s32[8,128]{1,0:T(8,128)} %bitcast.5, ...), custom_call_target="tpu_custom_call" | custom-call | flops 30000001024 | bytes 30000000 | tf_op jit(solution)/shard_map/pallas_call | solution.py:604
  173.1 1.8 %copy.10 = bf16[128,1792]{1,0:T(8,128)(2,1)} copy(bf16[128,1792]{1,0:T(8,128)(2,1)} %shard_map.82) | data formatting | bytes 917504

commit v4 on v3

--- a/solution.py
+++ b/solution.py
@@ -200,7 +200,8 @@
     summed = (cs[0, 1].astype(F32) + attention).astype(BF16)
     stream[...] = summed
     wide = summed.astype(F32)
-    ssb[0] = jnp.broadcast_to(jnp.sum(wide * wide, axis=1, keepdims=True), (tokens, META))
+    squares = jnp.sum(wide * wide, axis=1, keepdims=True)
+    ssb[0] = jnp.broadcast_to(squares, (tokens, META)).T[:8]
 
     def ss_copy(d):
         return remote(ssb.at[0], ssb.at[d], ss_s.at[d - 1], ss_r.at[d - 1], at(dy=d))
@@ -209,7 +210,8 @@
         ss_copy(d).start()
     for d in (1, 3, 2):
         ss_copy(d).wait_recv()
-    total = (ssb[0] + ssb[1] + ssb[2] + ssb[3])[:, :1]
+    total = ssb[0] + ssb[1] + ssb[2] + ssb[3]
+    total = jnp.broadcast_to(total[:1], (META, tokens)).T[:, :1]
     wide = stream[...].astype(F32)
     normed = wide * lax.rsqrt(total / width + 1e-06) * gain[...].reshape(1, quarter)
     toks[0, 0, c, :, pl.ds(0, quarter)] = normed.astype(BF16)
@@ -324,7 +326,7 @@
 
     def first_copy(j, q, outer, inner):
         dev = at(dx=inner * c, dz=inner * (1 - c))
-        return remote(cs.at[lax.rem(j, 3), q], fr.at[outer, inner - 1], f_s.at[lax.rem(j, 3), q], f_r.at[outer, inner - 1], dev)
+        return remote(cs.at[lax.rem(j, 4), q], fr.at[outer, inner - 1], f_s.at[lax.rem(j, 4), q], f_r.at[outer, inner - 1], dev)
 
     def second_copy(outer):
         dev = at(dx=outer * (1 - c), dz=outer * c)
@@ -406,9 +408,9 @@
     def gather_back(j):
         p_copy(j).wait()
         for q in range(2):
-            _, inner_before = place(j - 3, q)
-
-            @pl.when((j >= 3) & (inner_before != 0))
+            _, inner_before = place(j - 4, q)
+
+            @pl.when((j >= 4) & (inner_before != 0))
             def _():
                 first_copy(j, q, 0, 1).wait_send()
 
@@ -431,13 +433,13 @@
                 other = pr[lax.rem(j, 4), :, :, part].reshape(4 * cap, quarter // 2)
                 value = jnp.dot(sides[0], here, preferred_element_type=F32)
                 value = value + jnp.dot(sides[1], other, preferred_element_type=F32)
-                cs[lax.rem(j, 3), q, :, part] = value.astype(BF16)
+                cs[lax.rem(j, 4), q, :, part] = value.astype(BF16)
 
             outer, inner = place(j, q)
 
             @pl.when(inner == 0)
             def _():
-                own[outer] = cs[lax.rem(j, 3), q]
+                own[outer] = cs[lax.rem(j, 4), q]
 
             @pl.when(inner != 0)
             def _():
@@ -532,7 +534,7 @@
         pass_on(a, 1).wait_send()
         for b in range(4):
             core_copy(a, b).wait_send()
-    for j in (STEPS - 3, STEPS - 2, STEPS - 1):
+    for j in range(STEPS - 4, STEPS):
         for q in range(2):
             _, inner = place(j, q)
 
@@ -567,11 +569,11 @@
         pltpu.VMEM((2, local, 2, 2 * cap, quarter), BF16),
         pltpu.VMEM((4, local, 2 * cap, quarter), BF16),
         pltpu.VMEM((4, tokens, quarter), BF16),
-        pltpu.VMEM((3, 2, tokens, quarter), BF16),
+        pltpu.VMEM((4, 2, tokens, quarter), BF16),
         pltpu.VMEM((4, 3, tokens, quarter), BF16),
         pltpu.VMEM((3, tokens, quarter), BF16),
         pltpu.VMEM((tokens, quarter), BF16),
-        pltpu.VMEM((4, tokens, META), F32),
+        pltpu.VMEM((4, 8, tokens), F32),
         dma((18,)),
         dma((4,)),
         dma((2,)),
@@ -596,7 +598,7 @@
         dma((4, 3)),
         dma((2,)),
         dma((4,)),
-        dma((3, 2)),
+        dma((4, 2)),
         dma((4, 3)),
         dma((3,)),
         dma((3,)),
@@ -607,7 +609,7 @@
         in_specs=[anywhere, anywhere, vmem, anywhere, anywhere, vmem, vmem, vmem],
         out_specs=vmem,
         scratch_shapes=scratch,
-        compiler_params=pltpu.CompilerParams(collective_id=0, has_side_effects=True, vmem_limit_bytes=62 * 2**20),
+        compiler_params=pltpu.CompilerParams(collective_id=0, has_side_effects=True, vmem_limit_bytes=63 * 2**20),
         cost_estimate=pl.CostEstimate(flops=30 * 10**9, bytes_accessed=30 * 10**6, transcendentals=0),
     )(
         attn_partials[0],

time: 175 us -> 174 us (level)
  no operation moved by 1% of the time
where the time goes in v4:
time: 174 us
  Pallas kernels  172 us (99%)
  local copies, waits for them, and re-layouts  1.82 us (1%)
    pallas_call x1, Pallas kernels, per_device(): pl.pallas_call(functools.partial(layer_kernel, cap, groups * local), out_...  172 us

profile of v4, /device:TPU:1, one launch (start us, length us, event | category | flops | bytes accessed | tf_op | source)
XLA Modules:
  0.0 173.7 jit_solution(15070438266763267002)
XLA Ops:
  0.0 171.9 %shard_map.82 = bf16[128,1792]{1,0:T(8,128)(2,1)} custom-call(bf16[128,7168]{1,0:T(8,128)(2,1)} %bitcast.3, bf16[128,7168]{1,0:T(8,128)(2,1)} %resid.1, f32[1792]{0:T(1024)} %gain.1, bf16[2,1792,2048]{2,1,0:T(8,128)(2,1)} %wgu.1, bf16[2,1024,1792]{2,1,0:T(8,128)(2,1)} %wdn.1, s32[8,128]{1,0:T(8,128)} %bitcast.4, s32[8,128]{1,0:T(8,128)} %bitcast.5, ...), custom_call_target="tpu_custom_call" | custom-call | flops 30000001024 | bytes 30000000 | tf_op jit(solution)/shard_map/pallas_call | solution.py:606
  171.9 1.8 %copy.10 = bf16[128,1792]{1,0:T(8,128)(2,1)} copy(bf16[128,1792]{1,0:T(8,128)(2,1)} %shard_map.82) | data formatting | bytes 917504
